TPU v7x, 32 devices: a whole 2x2x4 slice. The times are simulated.
32 devices in a mesh: row: 8 (over z, y), col: 4 (over x, core).
Axes of the slice: x: 2, y: 2, z: 4, core: 2. Of those that a mesh axis runs over, the one named last changes fastest.
Arguments:
- train_points: float32 [16, 3, 8, 128], P(None, None, 'row'), may hold values from -6 to 6
- new_points: float32 [16, 256], replicated, may hold values from -6 to 6
- lengthscales: float32 [16], replicated, may hold values from 2.5 to 6
- factor: float32 [3, 8, 128, 3, 4, 256], P(None, 'row', None, None, 'col'), may hold values from -0.078125 to 0.078125
- diag_inverse: float32 [3, 8, 128, 4, 256], P(None, 'row', None, 'col'), may hold values from -3 to 3
Outputs:
- solution: float32 [3, 4, 8, 32, 256], P(None, 'col', 'row')
All inputs are finite; a program needn't handle non-finite values.
Results may differ from a plain program's by a relative error of at most 0.0001.
Values sent between devices are 32-bit elements; how exact they have to be, the bound alone decides.
A program may use at most 128 MiB of HBM per device.

v0:
```python
import jax
import jax.numpy as jnp
from jax import lax
from jax.sharding import PartitionSpec as P


def on_device(train_points, new_points, lengthscales, factor, diag_inverse):
    highest = lax.Precision.HIGHEST
    panels = factor.shape[0]
    block_rows = factor.shape[2]
    quarter_cols = factor.shape[5]
    new_count = new_points.shape[1]
    share_rows = block_rows // lax.axis_size("col")
    scaled_train = (train_points / lengthscales[:, None, None, None]).reshape(
        train_points.shape[0], panels * block_rows
    )
    scaled_new = new_points / lengthscales[:, None]
    inner_products = jnp.dot(scaled_train.T, scaled_new, precision=highest)
    sqdist = (
        jnp.sum(scaled_train * scaled_train, axis=0)[:, None]
        + jnp.sum(scaled_new * scaled_new, axis=0)[None, :]
        - 2.0 * inner_products
    )
    kernel = jnp.exp(-0.5 * sqdist).reshape(panels, block_rows, new_count)
    factor_blocks = factor.reshape(panels, block_rows, panels, quarter_cols)
    inverse_blocks = diag_inverse.reshape(panels, block_rows, quarter_cols)
    panel_numbers = jnp.arange(panels)

    def update(partial_rows, panel, quarter, after):
        column_slab = lax.dynamic_index_in_dim(factor_blocks, panel, axis=2, keepdims=False)
        change = jnp.einsum("piq,qm->pim", column_slab, quarter, precision=highest)
        below = (panel_numbers > after)[:, None, None]
        return partial_rows + jnp.where(below, change, 0.0)

    def advance(panel, loop_state):
        partial_rows, solved, pending = loop_state
        own_partial = lax.dynamic_index_in_dim(partial_rows, panel, 0, keepdims=False)
        summed = lax.psum(own_partial, "col")
        residual = lax.dynamic_index_in_dim(kernel, panel, 0, keepdims=False) - summed
        inverse_block = lax.dynamic_index_in_dim(inverse_blocks, panel, 0, keepdims=False)
        product = jnp.einsum("iq,im->qm", inverse_block, residual, precision=highest)
        own_rows = lax.psum_scatter(product, "row", scatter_dimension=0, tiled=True)
        quarter = lax.all_gather(own_rows, "row", axis=0, tiled=True)
        solved = lax.dynamic_update_index_in_dim(solved, own_rows, panel, 0)
        partial_rows = update(partial_rows, panel, quarter, panel)
        return (partial_rows, solved, pending)

    initial = (
        jnp.zeros((panels, block_rows, new_count), jnp.float32),
        jnp.zeros((panels, share_rows, new_count), jnp.float32),
        jnp.zeros((quarter_cols, new_count), jnp.float32),
    )
    partial_rows, solved, pending = lax.fori_loop(0, panels, advance, initial)
    return solved.reshape(panels, 1, 1, share_rows, new_count)


def solution(mesh):
    return jax.shard_map(
        on_device,
        mesh=mesh,
        in_specs=(
            P(None, None, "row", None),
            P(),
            P(),
            P(None, "row", None, None, "col", None),
            P(None, "row", None, "col", None),
        ),
        out_specs=P(None, "col", "row", None, None),
        check_vma=False,
    )
```

profile of v0, /device:TPU:0, one launch (start us, length us, event | category | flops | bytes accessed | tf_op | source)
XLA Modules:
  0.0 414.7 jit_solution(13480692311229317342)
XLA Ops:
  6.5 0.0 copy-start.1
  6.5 0.9 multiply_reduce_fusion.1
  7.4 0.9 fusion.17
  8.4 1.3 fusion.14
  9.6 1.0 copy.16
  10.7 0.0 copy-done.1
  10.7 0.1 copy.15
  10.8 397.0 %while.16 = (s32[]{:T(128)}, f32[3,128,256]{2,1,0:T(8,128)S(1)}, f32[3,32,256]{2,1,0:T(8,128)}, f32[3,128,3,256]{3,1,0,2:T(8,128)S(1)}, f32[3,128,256]{2,1,0:T(8...) while((s32[]{:T(128)}, f32[3,128,256]{2,1,0:T(8,128)S(1)}, ...), condition=%wide.region_5.6_spmd.clone, body=%wide.region_2.5_spmd.clone.sunk | while | flops 403013632 | bytes 5310182 | solution.py:53
  10.8 0.0 all-reduce.2.cloned.1.call-start
  10.9 0.7 dynamic-slice_bitcast_fusion.2
  11.6 0.0 all-reduce.2.cloned.1.call-update
  11.6 0.0 reduce-scatter.2.cloned.1.call-start
  11.6 36.5 %all-reduce.2.cloned.1.call-done = f32[128,256]{1,0:T(8,128)} async-done(((f32[128,256]{1,0:T(8,128)}), f32[128,256]{1,0:T(8,128)}) %all-reduce.2.cloned.1.call-update) | async-done | bytes 131088 | tf_op jit(solution)/shard_map/while/body/eval_jaxpr/psum | solution.py:38
  48.1 2.0 fusion.26
  50.1 0.0 reduce-scatter.2.cloned.1.call-update
  50.2 63.3 %reduce-scatter.2.cloned.1.call-done = f32[32,256]{1,0:T(8,128)} async-done(((f32[256,256]{1,0:T(8,128)}), f32[32,256]{1,0:T(8,128)}) %reduce-scatter.2.cloned.1.call-update) | async-done | bytes 32784 | tf_op jit(solution)/shard_map/while/body/eval_jaxpr/reduce_scatter | solution.py:42
  113.5 0.0 copy-start
  113.5 31.2 %all_gather.9 = f32[256,256]{1,0:T(8,128)S(1)} all-gather(f32[32,256]{1,0:T(8,128)} %reduce-scatter.2.cloned.1.call-done), channel_id=1, replica_groups=mesh['row'=8,'col'=4] {'row'}, dimensions={0}, use_global_device_ids=true | all-gather | bytes 294912 | tf_op jit(solution)/shard_map/while/body/eval_jaxpr/all_gather | solution.py:43
  144.7 0.5 fusion.27
  145.2 0.0 copy-done
  145.2 0.6 bitcast_dynamic-update-slice_fusion.2
  145.8 0.0 all-reduce.2.cloned.1.call-start
  145.9 0.7 dynamic-slice_bitcast_fusion.2
  146.5 0.0 all-reduce.2.cloned.1.call-update
  146.5 0.0 reduce-scatter.2.cloned.1.call-start
  146.6 32.7 %all-reduce.2.cloned.1.call-done = f32[128,256]{1,0:T(8,128)} async-done(((f32[128,256]{1,0:T(8,128)}), f32[128,256]{1,0:T(8,128)}) %all-reduce.2.cloned.1.call-update) | async-done | bytes 131088 | tf_op jit(solution)/shard_map/while/body/eval_jaxpr/psum | solution.py:38
  179.3 2.0 fusion.26
  181.3 0.0 reduce-scatter.2.cloned.1.call-update
  181.4 63.2 %reduce-scatter.2.cloned.1.call-done = f32[32,256]{1,0:T(8,128)} async-done(((f32[256,256]{1,0:T(8,128)}), f32[32,256]{1,0:T(8,128)}) %reduce-scatter.2.cloned.1.call-update) | async-done | bytes 32784 | tf_op jit(solution)/shard_map/while/body/eval_jaxpr/reduce_scatter | solution.py:42
  244.5 0.0 copy-start
  244.5 31.2 %all_gather.9 = f32[256,256]{1,0:T(8,128)S(1)} all-gather(f32[32,256]{1,0:T(8,128)} %reduce-scatter.2.cloned.1.call-done), channel_id=1, replica_groups=mesh['row'=8,'col'=4] {'row'}, dimensions={0}, use_global_device_ids=true | all-gather | bytes 294912 | tf_op jit(solution)/shard_map/while/body/eval_jaxpr/all_gather | solution.py:43
  275.8 0.5 fusion.27
  276.3 0.0 copy-done
  276.3 0.6 bitcast_dynamic-update-slice_fusion.2
  276.9 0.0 all-reduce.2.cloned.1.call-start
  276.9 0.7 dynamic-slice_bitcast_fusion.2
  277.6 0.0 all-reduce.2.cloned.1.call-update
  277.6 0.0 reduce-scatter.2.cloned.1.call-start
  277.7 32.6 %all-reduce.2.cloned.1.call-done = f32[128,256]{1,0:T(8,128)} async-done(((f32[128,256]{1,0:T(8,128)}), f32[128,256]{1,0:T(8,128)}) %all-reduce.2.cloned.1.call-update) | async-done | bytes 131088 | tf_op jit(solution)/shard_map/while/body/eval_jaxpr/psum | solution.py:38
  310.2 2.0 fusion.26
  312.3 0.0 reduce-scatter.2.cloned.1.call-update
  312.3 63.2 %reduce-scatter.2.cloned.1.call-done = f32[32,256]{1,0:T(8,128)} async-done(((f32[256,256]{1,0:T(8,128)}), f32[32,256]{1,0:T(8,128)}) %reduce-scatter.2.cloned.1.call-update) | async-done | bytes 32784 | tf_op jit(solution)/shard_map/while/body/eval_jaxpr/reduce_scatter | solution.py:42
  375.5 0.0 copy-start
  375.5 31.2 %all_gather.9 = f32[256,256]{1,0:T(8,128)S(1)} all-gather(f32[32,256]{1,0:T(8,128)} %reduce-scatter.2.cloned.1.call-done), channel_id=1, replica_groups=mesh['row'=8,'col'=4] {'row'}, dimensions={0}, use_global_device_ids=true | all-gather | bytes 294912 | tf_op jit(solution)/shard_map/while/body/eval_jaxpr/all_gather | solution.py:43
  406.7 0.5 fusion.27
  407.2 0.0 copy-done
  407.2 0.6 bitcast_dynamic-update-slice_fusion.2
  (8 shorter events, 0.1 us)
Async XLA Ops:
  6.5 4.2 %copy-start.1 = (f32[3,1,128,3,1,256]{5,4,3,2,1,0:T(1,128)S(1)}, f32[3,1,128,3,1,256]{5,4,3,2,1,0:T(1,128)}, u32[]{:S(2)}) copy-start(f32[3,1,128,3,1,256]{5,4,3,2,1,0:T(1,128)} %param.10) | copy-start | bytes 3538948
  10.8 37.3 %all-reduce.2.cloned.1.call-start = ((), (), s32[]{:S(2)}) async-start(), calls=%async_computation.1 | async-start | bytes 262144 | tf_op jit(solution)/shard_map/while/body/eval_jaxpr/psum | solution.py:38
  11.6 101.9 %reduce-scatter.2.cloned.1.call-start = ((), (), s32[]{:S(2)}) async-start(), calls=%async_computation.2 | async-start | bytes 294912 | tf_op jit(solution)/shard_map/while/body/eval_jaxpr/reduce_scatter | solution.py:42
  113.5 31.7 %copy-start = (f32[32,256]{1,0:T(8,128)S(1)}, f32[32,256]{1,0:T(8,128)}, u32[]{:S(2)}) copy-start(f32[32,256]{1,0:T(8,128)} %reduce-scatter.2.cloned.1.call-done) | copy-start | bytes 98308 | tf_op jit(solution)/shard_map/while
  145.8 33.5 %all-reduce.2.cloned.1.call-start = ((), (), s32[]{:S(2)}) async-start(), calls=%async_computation.1 | async-start | bytes 262144 | tf_op jit(solution)/shard_map/while/body/eval_jaxpr/psum | solution.py:38
  146.5 98.0 %reduce-scatter.2.cloned.1.call-start = ((), (), s32[]{:S(2)}) async-start(), calls=%async_computation.2 | async-start | bytes 294912 | tf_op jit(solution)/shard_map/while/body/eval_jaxpr/reduce_scatter | solution.py:42
  244.5 31.7 %copy-start = (f32[32,256]{1,0:T(8,128)S(1)}, f32[32,256]{1,0:T(8,128)}, u32[]{:S(2)}) copy-start(f32[32,256]{1,0:T(8,128)} %reduce-scatter.2.cloned.1.call-done) | copy-start | bytes 98308 | tf_op jit(solution)/shard_map/while
  276.9 33.3 %all-reduce.2.cloned.1.call-start = ((), (), s32[]{:S(2)}) async-start(), calls=%async_computation.1 | async-start | bytes 262144 | tf_op jit(solution)/shard_map/while/body/eval_jaxpr/psum | solution.py:38
  277.6 97.8 %reduce-scatter.2.cloned.1.call-start = ((), (), s32[]{:S(2)}) async-start(), calls=%async_computation.2 | async-start | bytes 294912 | tf_op jit(solution)/shard_map/while/body/eval_jaxpr/reduce_scatter | solution.py:42
  375.5 31.7 %copy-start = (f32[32,256]{1,0:T(8,128)S(1)}, f32[32,256]{1,0:T(8,128)}, u32[]{:S(2)}) copy-start(f32[32,256]{1,0:T(8,128)} %reduce-scatter.2.cloned.1.call-done) | copy-start | bytes 98308 | tf_op jit(solution)/shard_map/while
Sparse Core Ops, SparseCore 0:
  14.0 34.0 all-reduce.1
  51.8 61.6 reduce-scatter.1
  149.0 30.3 all-reduce.1
  182.9 61.6 reduce-scatter.1
  279.7 30.4 all-reduce.1
  313.8 61.6 reduce-scatter.1
where the time goes:
time: 415 us
  waiting for transfers between devices  292 us (70%)
  blocking collectives  93.7 us (23%)
  between operations  13.4 us (3%)
  matrix products  8.75 us (2%)
  local copies, waits for them, and re-layouts  4.98 us (1%)
    reduce_scatter x3, waiting for transfers between devices, advance(): own_rows = lax.psum_scatter(product, 'row', scatter_dimension=0, tiled=True)  190 us
    psum x3, waiting for transfers between devices, advance(): summed = lax.psum(own_partial, 'col')  102 us
    all_gather x3, blocking collectives, advance(): quarter = lax.all_gather(own_rows, 'row', axis=0, tiled=True)  93.7 us
  transfers between devices with their start and end apart: 6, of which 6 were waited for; matrix products, arithmetic and copies ran while one was open for 0% of the time, Pallas kernels for 0%

commit v1 on v0

v1 whole, which is shorter than its diff:
```python
import functools

import jax
import jax.numpy as jnp
from jax import lax
from jax.experimental import pallas as pl
from jax.experimental.pallas import tpu as pltpu
from jax.sharding import PartitionSpec as P

MESH = pl.DeviceIdType.MESH
HIGHEST = lax.Precision.HIGHEST
HALVES = 2


def dot(a, b):
    return jnp.dot(a, b, precision=HIGHEST, preferred_element_type=jnp.float32)


def blocks_below(panels):
    return [(k, j) for k in range(panels) for j in range(k)]


def kernel(
    n_row, n_col, panels, dims, unit,
    train_ref, new_ref, lens_ref, l_ref, w_ref, out_ref,
    train_peer, l_peer, w_cat, w_send, k_ref, r_buf, p_buf, p_in, x_buf, s_buf, s_in, acc,
    send_sem, recv_sem, pre_send, pre_recv,
):
    row, col = lax.axis_index("row"), lax.axis_index("col")
    n_s = n_row // 2
    s, t = row // 2, row % 2
    width = w_ref.shape[2]
    block_rows = w_ref.shape[1]
    mw = r_buf.shape[3]
    below = blocks_below(panels)
    pair = (2 * s + (1 - t), col)
    s_peers = [(d, (2 * ((s + d) % n_s) + t, col)) for d in range(1, n_s)]
    q_offsets = [(dt, dc) for dt in range(2) for dc in range(n_col) if dt + dc > 0]
    q_peers = [
        (dt, dc, (2 * s + (t + dt) % 2, (col + dc) % n_col)) for dt, dc in q_offsets
    ]

    barrier = pltpu.get_barrier_semaphore()
    for device in [p[-1] for p in s_peers] + [p[-1] for p in q_peers]:
        pl.semaphore_signal(barrier, inc=1, device_id=device, device_id_type=MESH)

    def rows(number):
        return pl.ds(pl.multiple_of(number * unit, unit), unit)

    def wait(ref, sem):
        pltpu.make_async_copy(ref, ref, sem).wait()

    def pair_copy(src, dst, number):
        return pltpu.make_async_remote_copy(
            src_ref=src, dst_ref=dst, send_sem=pre_send.at[number], recv_sem=pre_recv.at[number],
            device_id=pair, device_id_type=MESH,
        )

    copies = [pair_copy(train_ref, train_peer, 0)]
    for k in range(panels):
        copies.append(pair_copy(w_send.at[k], w_cat.at[k, :, pl.ds(block_rows, block_rows)], 1 + k))
    for b in range(len(below)):
        copies.append(pair_copy(l_ref.at[b], l_peer.at[b], 1 + panels + b))

    def split_inverse(k):
        for b in range(width // 128):
            turned = w_ref[k, :, b * 128:(b + 1) * 128].T
            even = [turned[i * unit:(i + 1) * unit] for i in range(0, 128 // unit, 2)]
            odd = [turned[i * unit:(i + 1) * unit] for i in range(1, 128 // unit, 2)]
            even, odd = jnp.concatenate(even, axis=0), jnp.concatenate(odd, axis=0)
            w_cat[k, b * 64:(b + 1) * 64, 0:block_rows] = jnp.where(t == 0, even, odd)
            w_send[k, b * 64:(b + 1) * 64, :] = jnp.where(t == 0, odd, even)

    split_inverse(0)
    pl.semaphore_wait(barrier, len(s_peers) + len(q_peers))
    copies[0].start()
    copies[1].start()
    for k in range(1, panels):
        split_inverse(k)
    order = []
    for b, (k, j) in enumerate(below):
        if j == 0:
            order.append(1 + k)
        order.append(1 + panels + b)
    for number in order:
        copies[number].start()

    diagonal = lax.broadcasted_iota(jnp.int32, (dims, dims), 0) == lax.broadcasted_iota(
        jnp.int32, (dims, dims), 1
    )
    lens = jnp.sum(
        jnp.where(diagonal, jnp.broadcast_to(lens_ref[...], (dims, dims)), 0.0), axis=1, keepdims=True
    )
    scaled_new = new_ref[...] / lens
    new_square = jnp.sum(scaled_new * scaled_new, axis=0, keepdims=True)

    def kernel_rows(points):
        turned = (points / lens).T
        square = jnp.sum(turned * turned, axis=1, keepdims=True)
        return jnp.exp(-0.5 * (square + new_square - 2.0 * dot(turned, scaled_new)))

    def panel_points(ref, k):
        return ref[pl.ds(k, dims, stride=panels), :]

    own = kernel_rows(panel_points(train_ref, 0))
    for h in range(HALVES):
        r_buf[0, h, 0:block_rows, :] = own[:, h * mw:(h + 1) * mw]
    for k in range(1, panels):
        k_ref[k] = kernel_rows(panel_points(train_ref, k))

    for k in range(panels - 1):
        for h in range(HALVES):
            for i in range(n_s):
                x_buf[k, h, rows(2 * i + 1 - t), :] = jnp.zeros((unit, mw), jnp.float32)

    copies[0].wait_recv()
    other = kernel_rows(panel_points(train_peer, 0))
    for h in range(HALVES):
        r_buf[0, h, block_rows:2 * block_rows, :] = other[:, h * mw:(h + 1) * mw]

    def sem_of(stage, k, h):
        return (stage * panels + k) * HALVES + h

    def send(stage, k, h, src, dst, device):
        number = sem_of(stage, k, h)
        pltpu.make_async_remote_copy(
            src_ref=src, dst_ref=dst, send_sem=send_sem.at[number], recv_sem=recv_sem.at[number],
            device_id=device, device_id_type=MESH,
        ).start()

    s_rows = pl.ds(0, len(s_peers) * unit)
    q_rows = pl.ds(0, len(q_peers) * unit)

    def apply_inverse(k, h):
        if k > 0:
            wait(r_buf.at[k, h, q_rows], recv_sem.at[sem_of(3, k - 1, h)])
        p_buf[k, h] = dot(w_cat[k], r_buf[k, h])
        for d, device in s_peers:
            send(0, k, h, p_buf.at[k, h, rows((s + d) % n_s)], p_in.at[k, h, rows(d - 1)], device)

    def sum_solved(k, h):
        wait(p_in.at[k, h, s_rows], recv_sem.at[sem_of(0, k, h)])
        total = p_buf[k, h, rows(s), :]
        for d in range(n_s - 1):
            total = total + p_in[k, h, d * unit:(d + 1) * unit, :]
        out_ref[k, :, h * mw:(h + 1) * mw] = total
        if k < panels - 1:
            x_buf[k, h, rows(row), :] = total
            for d, device in s_peers:
                send(1, k, h, x_buf.at[k, h, rows(row)], x_buf.at[k, h, rows(row)], device)

    def apply_factor(k, h):
        wait(x_buf.at[k, h, s_rows], recv_sem.at[sem_of(1, k, h)])
        x = x_buf[k, h]
        b = below.index((k + 1, k))
        for side, ref in enumerate((l_ref, l_peer)):
            change = dot(ref[b], x)
            part = pl.ds(side * block_rows, block_rows)
            s_buf[k, h, part, :] = change + acc[k + 1, h, part, :] if k > 0 else change
        for number, (dt, dc, device) in enumerate(q_peers):
            source = rows(dt * n_col + (col + dc) % n_col)
            send(2, k, h, s_buf.at[k, h, source], s_in.at[k, h, rows(number)], device)

    def look_ahead(k, h):
        x = x_buf[k, h]
        for later in range(k + 2, panels):
            b = below.index((later, k))
            for side, ref in enumerate((l_ref, l_peer)):
                change = dot(ref[b], x)
                part = pl.ds(side * block_rows, block_rows)
                acc[later, h, part, :] = change + acc[later, h, part, :] if k > 0 else change

    def sum_residual(k, h):
        wait(s_in.at[k, h, q_rows], recv_sem.at[sem_of(2, k, h)])
        total = s_buf[k, h, rows(col), :]
        for number in range(len(q_peers)):
            total = total + s_in[k, h, number * unit:(number + 1) * unit, :]
        r_buf[k + 1, h, rows(col), :] = k_ref[k + 1, rows(col), h * mw:(h + 1) * mw] - total
        for dt, dc, device in q_peers:
            send(
                3, k, h, r_buf.at[k + 1, h, rows(col)], r_buf.at[k + 1, h, rows(dt * n_col + col)], device
            )

    for k in range(panels):
        copies[1 + k].wait_recv()
        for h in range(HALVES):
            apply_inverse(k, h)
        for h in range(HALVES):
            sum_solved(k, h)
        if k < panels - 1:
            copies[1 + panels + below.index((k + 1, k))].wait_recv()
            for h in range(HALVES):
                apply_factor(k, h)
            for later in range(k + 2, panels):
                copies[1 + panels + below.index((later, k))].wait_recv()
            for h in range(HALVES):
                look_ahead(k, h)
            for h in range(HALVES):
                sum_residual(k, h)

    for copy in copies:
        copy.wait_send()
    for k in range(panels):
        for h in range(HALVES):
            wait(p_in.at[k, h, s_rows], send_sem.at[sem_of(0, k, h)])
            if k < panels - 1:
                wait(p_in.at[k, h, s_rows], send_sem.at[sem_of(1, k, h)])
                wait(s_in.at[k, h, q_rows], send_sem.at[sem_of(2, k, h)])
                wait(s_in.at[k, h, q_rows], send_sem.at[sem_of(3, k, h)])


def on_device(train_points, new_points, lengthscales, factor, diag_inverse):
    n_row, n_col = lax.axis_size("row"), lax.axis_size("col")
    panels, _, block_rows = factor.shape[:3]
    width = factor.shape[5]
    dims, new_count = new_points.shape
    unit = block_rows // n_col
    n_s = n_row // 2
    mw = new_count // HALVES
    below = blocks_below(panels)
    train = train_points.reshape(dims * panels, block_rows)
    lower = jnp.stack([factor[k, 0, :, j, 0, :] for k, j in below])
    inverse = diag_inverse.reshape(panels, block_rows, width)
    f32 = jnp.float32
    scratch = [
        pltpu.VMEM((dims * panels, block_rows), f32),
        pltpu.VMEM((len(below), block_rows, width), f32),
        pltpu.VMEM((panels, width // 2, 2 * block_rows), f32),
        pltpu.VMEM((panels, width // 2, block_rows), f32),
        pltpu.VMEM((panels, block_rows, new_count), f32),
        pltpu.VMEM((panels, HALVES, 2 * block_rows, mw), f32),
        pltpu.VMEM((panels, HALVES, width // 2, mw), f32),
        pltpu.VMEM((panels, HALVES, (n_s - 1) * unit, mw), f32),
        pltpu.VMEM((panels - 1, HALVES, width, mw), f32),
        pltpu.VMEM((panels - 1, HALVES, 2 * block_rows, mw), f32),
        pltpu.VMEM((panels - 1, HALVES, (2 * n_col - 1) * unit, mw), f32),
        pltpu.VMEM((panels, HALVES, 2 * block_rows, mw), f32),
        pltpu.SemaphoreType.DMA((4 * panels * HALVES,)),
        pltpu.SemaphoreType.DMA((4 * panels * HALVES,)),
        pltpu.SemaphoreType.DMA((1 + panels + len(below),)),
        pltpu.SemaphoreType.DMA((1 + panels + len(below),)),
    ]
    solved = pl.pallas_call(
        functools.partial(kernel, n_row, n_col, panels, dims, unit),
        out_shape=jax.ShapeDtypeStruct((panels, unit, new_count), f32),
        in_specs=[pl.BlockSpec(memory_space=pltpu.VMEM)] * 5,
        out_specs=pl.BlockSpec(memory_space=pltpu.VMEM),
        scratch_shapes=scratch,
        compiler_params=pltpu.CompilerParams(
            collective_id=0, has_side_effects=True,
            vmem_limit_bytes=(12 << 20) + 44 * block_rows * width * 4,
        ),
        cost_estimate=pl.CostEstimate(
            flops=12 * block_rows * width * new_count * panels,
            bytes_accessed=8 * panels * block_rows * width * 4,
            transcendentals=panels * block_rows * new_count,
        ),
    )(train, new_points, lengthscales.reshape(1, dims), lower, inverse)
    return solved.reshape(panels, 1, 1, unit, new_count)


def solution(mesh):
    return jax.shard_map(
        on_device,
        mesh=mesh,
        in_specs=(
            P(None, None, "row", None),
            P(),
            P(),
            P(None, "row", None, None, "col", None),
            P(None, "row", None, "col", None),
        ),
        out_specs=P(None, "col", "row", None, None),
        check_vma=False,
    )
```

time: 415 us -> 51.5 us (0.12)
  waiting for transfers between devices: 292 us -> 0 us
  blocking collectives: 93.7 us -> 0 us
  Pallas kernels: 0 us -> 48.6 us
  between operations: 13.4 us -> 0.08 us
  matrix products: 8.75 us -> 0 us
    reduce_scatter x3 -> x0, waiting for transfers between devices: 190 us -> none  [advance(): own_rows = lax.psum_scatter(product, 'row', scatter_dimension=0, tiled=True)]
    psum x3 -> x0, waiting for transfers between devices: 102 us -> none  [advance(): summed = lax.psum(own_partial, 'col')]
    all_gather x3 -> x0, blocking collectives: 93.7 us -> none  [advance(): quarter = lax.all_gather(own_rows, 'row', axis=0, tiled=True)]
    pallas_call x0 -> x1, Pallas kernels: none -> 48.6 us  [on_device(): pl.pallas_call(functools.partial(kernel, n_row, n_col, panels, dims, unit...]
    dot_general x7 -> x0, matrix products: 8.75 us -> none  [the longest x3 6.03 us: advance(): jnp.einsum('iq,im->qm', inverse_block, residual, precision=highest)]
  transfers between devices with their start and end apart: 6 -> 0, of which waited for: 6 -> 0; matrix products, arithmetic and copies ran while one was open for 0% -> 0% of each run, Pallas kernels for 0% -> 0%
where the time goes in v1:
time: 51.5 us; the launch traced here: 51.3 us
  Pallas kernels  48.6 us (94%)
  local copies, waits for them, and re-layouts  2.65 us (5%)
    pallas_call x1, Pallas kernels, on_device(): pl.pallas_call(functools.partial(kernel, n_row, n_col, panels, dims, unit...  48.6 us
    slice x1, local copies, waits for them, and re-layouts, on_device(): lower = jnp.stack([factor[k, 0, :, j, 0, :] for k, j in below])  1.35 us
    unnamed x11, local copies, waits for them, and re-layouts  1.28 us

profile of v1, /device:TPU:0, one launch (start us, length us, event | category | flops | bytes accessed | tf_op | source)
XLA Modules:
  0.0 51.3 jit_solution(332262651005233003)
XLA Ops:
  0.0 0.0 copy-start.3
  0.0 1.4 %fusion = (f32[1,1,128,1,1,256]{5,4,3,2,1,0:T(1,128)S(1)}, f32[1,1,128,1,1,256]{5,4,3,2,1,0:T(1,128)S(1)}, f32[1,1,128,1,1,256]{5,4,3,2,1,0:T(1,128)S(1)}) fusion(f32[3,1,128,3,1,256]{5,4,3,2,1,0:T(1,128)} %param.8), kind=kLoop, calls=%fused_computation.5 | loop fusion | bytes 786432 | tf_op jit(solution)/shard_map/slice | solution.py:222
  1.4 0.0 copy-start
  1.4 0.0 copy-start.1
  1.4 0.0 copy-start.2
  1.5 0.0 copy-done.3
  1.5 0.6 %copy-done = f32[16,3,1,128]{3,2,1,0:T(1,128)S(1)} copy-done((f32[16,3,1,128]{3,2,1,0:T(1,128)S(1)}, f32[16,3,1,128]{3,2,1,0:T(1,128)}, u32[]{:S(2)}) %copy-start) | copy-done | bytes 24600
  2.1 0.0 copy-done.1
  2.1 0.0 copy-done.2
  2.1 48.6 %shard_map.55 = f32[3,32,256]{2,1,0:T(8,128)S(1)} custom-call(f32[48,128]{1,0:T(8,128)S(1)} %bitcast.17, f32[16,256]{1,0:T(8,128)S(1)} %copy-done.1, f32[1,16]{1,0:T(1,128)S(1)} %bitcast.18, f32[3,128,256]{2,1,0:T(8,128)S(1)} %pad_maximum_fusion.l_ref, f32[3,128,256]{2,1,0:T(8,128)S(1)} %bitcast.15), custom_call_target="tpu_custom_call" | custom-call | flops 301989888 | bytes 3145728 | tf_op jit(solution)/shard_map/pallas_call | solution.py:243
  50.7 0.6 %copy.21 = f32[3,1,1,32,256]{4,3,2,1,0:T(8,128)} copy(f32[3,1,1,32,256]{4,3,2,1,0:T(8,128)S(1)} %bitcast.16) | data formatting | bytes 196608
  (4 shorter events, 0.1 us)
Async XLA Ops:
  0.0 1.5 %copy-start.3 = (f32[3,1,128,1,256]{4,3,2,1,0:T(1,128)S(1)}, f32[3,1,128,1,256]{4,3,2,1,0:T(1,128)}, u32[]{:S(2)}) copy-start(f32[3,1,128,1,256]{4,3,2,1,0:T(1,128)} %param.9) | copy-start | bytes 1179652
  1.4 0.7 %copy-start = (f32[16,3,1,128]{3,2,1,0:T(1,128)S(1)}, f32[16,3,1,128]{3,2,1,0:T(1,128)}, u32[]{:S(2)}) copy-start(f32[16,3,1,128]{3,2,1,0:T(1,128)} %param.5) | copy-start | bytes 73732
  1.4 0.7 %copy-start.1 = (f32[16,256]{1,0:T(8,128)S(1)}, f32[16,256]{1,0:T(8,128)}, u32[]{:S(2)}) copy-start(f32[16,256]{1,0:T(8,128)} %new_ref.1) | copy-start | bytes 49156
  1.4 0.7 %copy-start.2 = (f32[16]{0:T(128)S(1)}, f32[16]{0:T(128)}, u32[]{:S(2)}) copy-start(f32[16]{0:T(128)} %param.7) | copy-start | bytes 196

commit v2 on v1

--- a/solution.py
+++ b/solution.py
@@ -16,6 +16,19 @@
     return jnp.dot(a, b, precision=HIGHEST, preferred_element_type=jnp.float32)
 
 
+def split(a):
+    high = a.astype(jnp.bfloat16)
+    return high, (a - high.astype(jnp.float32)).astype(jnp.bfloat16)
+
+
+def dot_split(a_high, a_low, b):
+    high, low = split(b)
+    wide = jnp.dot(a_high, jnp.concatenate([high, low], axis=1), preferred_element_type=jnp.float32)
+    cross = jnp.dot(a_low, high, preferred_element_type=jnp.float32)
+    n = b.shape[1]
+    return wide[:, :n] + (wide[:, n:] + cross)
+
+
 def blocks_below(panels):
     return [(k, j) for k in range(panels) for j in range(k)]
 
@@ -23,7 +36,7 @@
 def kernel(
     n_row, n_col, panels, dims, unit,
     train_ref, new_ref, lens_ref, l_ref, w_ref, out_ref,
-    train_peer, l_peer, w_cat, w_send, k_ref, r_buf, p_buf, p_in, x_buf, s_buf, s_in, acc,
+    train_peer, l_peer, w_peer, w_send, w_high, w_low, l_high, l_low, k_ref, r_buf, p_buf, p_in, x_buf, s_buf, s_in, acc,
     send_sem, recv_sem, pre_send, pre_recv,
 ):
     row, col = lax.axis_index("row"), lax.axis_index("col")
@@ -58,7 +71,7 @@
 
     copies = [pair_copy(train_ref, train_peer, 0)]
     for k in range(panels):
-        copies.append(pair_copy(w_send.at[k], w_cat.at[k, :, pl.ds(block_rows, block_rows)], 1 + k))
+        copies.append(pair_copy(w_send.at[k], w_peer.at[k], 1 + k))
     for b in range(len(below)):
         copies.append(pair_copy(l_ref.at[b], l_peer.at[b], 1 + panels + b))
 
@@ -68,10 +81,47 @@
             even = [turned[i * unit:(i + 1) * unit] for i in range(0, 128 // unit, 2)]
             odd = [turned[i * unit:(i + 1) * unit] for i in range(1, 128 // unit, 2)]
             even, odd = jnp.concatenate(even, axis=0), jnp.concatenate(odd, axis=0)
-            w_cat[k, b * 64:(b + 1) * 64, 0:block_rows] = jnp.where(t == 0, even, odd)
+            high, low = split(jnp.where(t == 0, even, odd))
+            w_high[k, b * 64:(b + 1) * 64, 0:block_rows] = high
+            w_low[k, b * 64:(b + 1) * 64, 0:block_rows] = low
             w_send[k, b * 64:(b + 1) * 64, :] = jnp.where(t == 0, odd, even)
 
+    def keep_block(b, side, ref):
+        high, low = split(ref[b])
+        l_high[b, side * block_rows:(side + 1) * block_rows, :] = high
+        l_low[b, side * block_rows:(side + 1) * block_rows, :] = low
+
+    def take_block(b):
+        copies[1 + panels + b].wait_recv()
+        keep_block(b, 1, l_peer)
+
+    def take_inverse(k):
+        copies[1 + k].wait_recv()
+        high, low = split(w_peer[k])
+        w_high[k, :, block_rows:2 * block_rows] = high
+        w_low[k, :, block_rows:2 * block_rows] = low
+
     split_inverse(0)
+    diagonal = lax.broadcasted_iota(jnp.int32, (dims, dims), 0) == lax.broadcasted_iota(
+        jnp.int32, (dims, dims), 1
+    )
+    lens = jnp.sum(
+        jnp.where(diagonal, jnp.broadcast_to(lens_ref[...], (dims, dims)), 0.0), axis=1, keepdims=True
+    )
+    scaled_new = new_ref[...] / lens
+    new_square = jnp.sum(scaled_new * scaled_new, axis=0, keepdims=True)
+
+    def kernel_rows(points):
+        turned = (points / lens).T
+        square = jnp.sum(turned * turned, axis=1, keepdims=True)
+        return jnp.exp(-0.5 * (square + new_square - 2.0 * dot(turned, scaled_new)))
+
+    def panel_points(ref, k):
+        return ref[pl.ds(k, dims, stride=panels), :]
+
+    own = kernel_rows(panel_points(train_ref, 0))
+    for h in range(HALVES):
+        r_buf[0, h, 0:block_rows, :] = own[:, h * mw:(h + 1) * mw]
     pl.semaphore_wait(barrier, len(s_peers) + len(q_peers))
     copies[0].start()
     copies[1].start()
@@ -85,26 +135,6 @@
     for number in order:
         copies[number].start()
 
-    diagonal = lax.broadcasted_iota(jnp.int32, (dims, dims), 0) == lax.broadcasted_iota(
-        jnp.int32, (dims, dims), 1
-    )
-    lens = jnp.sum(
-        jnp.where(diagonal, jnp.broadcast_to(lens_ref[...], (dims, dims)), 0.0), axis=1, keepdims=True
-    )
-    scaled_new = new_ref[...] / lens
-    new_square = jnp.sum(scaled_new * scaled_new, axis=0, keepdims=True)
-
-    def kernel_rows(points):
-        turned = (points / lens).T
-        square = jnp.sum(turned * turned, axis=1, keepdims=True)
-        return jnp.exp(-0.5 * (square + new_square - 2.0 * dot(turned, scaled_new)))
-
-    def panel_points(ref, k):
-        return ref[pl.ds(k, dims, stride=panels), :]
-
-    own = kernel_rows(panel_points(train_ref, 0))
-    for h in range(HALVES):
-        r_buf[0, h, 0:block_rows, :] = own[:, h * mw:(h + 1) * mw]
     for k in range(1, panels):
         k_ref[k] = kernel_rows(panel_points(train_ref, k))
 
@@ -112,6 +142,9 @@
         for h in range(HALVES):
             for i in range(n_s):
                 x_buf[k, h, rows(2 * i + 1 - t), :] = jnp.zeros((unit, mw), jnp.float32)
+
+    for b in range(len(below)):
+        keep_block(b, 0, l_ref)
 
     copies[0].wait_recv()
     other = kernel_rows(panel_points(train_peer, 0))
@@ -134,7 +167,7 @@
     def apply_inverse(k, h):
         if k > 0:
             wait(r_buf.at[k, h, q_rows], recv_sem.at[sem_of(3, k - 1, h)])
-        p_buf[k, h] = dot(w_cat[k], r_buf[k, h])
+        p_buf[k, h] = dot_split(w_high[k], w_low[k], r_buf[k, h])
         for d, device in s_peers:
             send(0, k, h, p_buf.at[k, h, rows((s + d) % n_s)], p_in.at[k, h, rows(d - 1)], device)
 
@@ -153,10 +186,8 @@
         wait(x_buf.at[k, h, s_rows], recv_sem.at[sem_of(1, k, h)])
         x = x_buf[k, h]
         b = below.index((k + 1, k))
-        for side, ref in enumerate((l_ref, l_peer)):
-            change = dot(ref[b], x)
-            part = pl.ds(side * block_rows, block_rows)
-            s_buf[k, h, part, :] = change + acc[k + 1, h, part, :] if k > 0 else change
+        change = dot_split(l_high[b], l_low[b], x)
+        s_buf[k, h] = change + acc[k + 1, h] if k > 0 else change
         for number, (dt, dc, device) in enumerate(q_peers):
             source = rows(dt * n_col + (col + dc) % n_col)
             send(2, k, h, s_buf.at[k, h, source], s_in.at[k, h, rows(number)], device)
@@ -165,10 +196,8 @@
         x = x_buf[k, h]
         for later in range(k + 2, panels):
             b = below.index((later, k))
-            for side, ref in enumerate((l_ref, l_peer)):
-                change = dot(ref[b], x)
-                part = pl.ds(side * block_rows, block_rows)
-                acc[later, h, part, :] = change + acc[later, h, part, :] if k > 0 else change
+            change = dot_split(l_high[b], l_low[b], x)
+            acc[later, h] = change + acc[later, h] if k > 0 else change
 
     def sum_residual(k, h):
         wait(s_in.at[k, h, q_rows], recv_sem.at[sem_of(2, k, h)])
@@ -181,18 +210,20 @@
                 3, k, h, r_buf.at[k + 1, h, rows(col)], r_buf.at[k + 1, h, rows(dt * n_col + col)], device
             )
 
+    take_inverse(0)
     for k in range(panels):
-        copies[1 + k].wait_recv()
         for h in range(HALVES):
             apply_inverse(k, h)
+        if k < panels - 1:
+            take_block(below.index((k + 1, k)))
         for h in range(HALVES):
             sum_solved(k, h)
         if k < panels - 1:
-            copies[1 + panels + below.index((k + 1, k))].wait_recv()
             for h in range(HALVES):
                 apply_factor(k, h)
+            take_inverse(k + 1)
             for later in range(k + 2, panels):
-                copies[1 + panels + below.index((later, k))].wait_recv()
+                take_block(below.index((later, k)))
             for h in range(HALVES):
                 look_ahead(k, h)
             for h in range(HALVES):
@@ -225,8 +256,12 @@
     scratch = [
         pltpu.VMEM((dims * panels, block_rows), f32),
         pltpu.VMEM((len(below), block_rows, width), f32),
-        pltpu.VMEM((panels, width // 2, 2 * block_rows), f32),
         pltpu.VMEM((panels, width // 2, block_rows), f32),
+        pltpu.VMEM((panels, width // 2, block_rows), f32),
+        pltpu.VMEM((panels, width // 2, 2 * block_rows), jnp.bfloat16),
+        pltpu.VMEM((panels, width // 2, 2 * block_rows), jnp.bfloat16),
+        pltpu.VMEM((len(below), 2 * block_rows, width), jnp.bfloat16),
+        pltpu.VMEM((len(below), 2 * block_rows, width), jnp.bfloat16),
         pltpu.VMEM((panels, block_rows, new_count), f32),
         pltpu.VMEM((panels, HALVES, 2 * block_rows, mw), f32),
         pltpu.VMEM((panels, HALVES, width // 2, mw), f32),

time: 51.5 us -> 51 us (level)
  Pallas kernels: 48.6 us -> 48 us
    pallas_call x1, Pallas kernels: 48.6 us -> 48 us  [on_device(): pl.pallas_call(functools.partial(kernel, n_row, n_col, panels, dims, unit...]
where the time goes in v2:
time: 51 us; the launch traced here: 50.8 us
  Pallas kernels  48 us (94%)
  local copies, waits for them, and re-layouts  2.65 us (5%)
    pallas_call x1, Pallas kernels, on_device(): pl.pallas_call(functools.partial(kernel, n_row, n_col, panels, dims, unit...  48 us
    slice x1, local copies, waits for them, and re-layouts, on_device(): lower = jnp.stack([factor[k, 0, :, j, 0, :] for k, j in below])  1.35 us
    unnamed x11, local copies, waits for them, and re-layouts  1.28 us

profile of v2, /device:TPU:0, one launch (start us, length us, event | category | flops | bytes accessed | tf_op | source)
XLA Modules:
  0.0 50.8 jit_solution(18089156289439710090)
XLA Ops:
  0.0 0.0 copy-start.3
  0.0 1.4 %fusion = (f32[1,1,128,1,1,256]{5,4,3,2,1,0:T(1,128)S(1)}, f32[1,1,128,1,1,256]{5,4,3,2,1,0:T(1,128)S(1)}, f32[1,1,128,1,1,256]{5,4,3,2,1,0:T(1,128)S(1)}) fusion(f32[3,1,128,3,1,256]{5,4,3,2,1,0:T(1,128)} %param.8), kind=kLoop, calls=%fused_computation.5 | loop fusion | bytes 786432 | tf_op jit(solution)/shard_map/slice | solution.py:253
  1.4 0.0 copy-start
  1.4 0.0 copy-start.1
  1.4 0.0 copy-start.2
  1.5 0.0 copy-done.3
  1.5 0.6 %copy-done = f32[16,3,1,128]{3,2,1,0:T(1,128)S(1)} copy-done((f32[16,3,1,128]{3,2,1,0:T(1,128)S(1)}, f32[16,3,1,128]{3,2,1,0:T(1,128)}, u32[]{:S(2)}) %copy-start) | copy-done | bytes 24600
  2.1 0.0 copy-done.1
  2.1 0.0 copy-done.2
  2.1 48.0 %shard_map.55 = f32[3,32,256]{2,1,0:T(8,128)S(1)} custom-call(f32[48,128]{1,0:T(8,128)S(1)} %bitcast.17, f32[16,256]{1,0:T(8,128)S(1)} %copy-done.1, f32[1,16]{1,0:T(1,128)S(1)} %bitcast.18, f32[3,128,256]{2,1,0:T(8,128)S(1)} %pad_maximum_fusion.l_ref, f32[3,128,256]{2,1,0:T(8,128)S(1)} %bitcast.15), custom_call_target="tpu_custom_call" | custom-call | flops 301989888 | bytes 3145728 | tf_op jit(solution)/shard_map/pallas_call | solution.py:278
  50.1 0.6 %copy.21 = f32[3,1,1,32,256]{4,3,2,1,0:T(8,128)} copy(f32[3,1,1,32,256]{4,3,2,1,0:T(8,128)S(1)} %bitcast.16) | data formatting | bytes 196608
  (4 shorter events, 0.1 us)
Async XLA Ops:
  0.0 1.5 %copy-start.3 = (f32[3,1,128,1,256]{4,3,2,1,0:T(1,128)S(1)}, f32[3,1,128,1,256]{4,3,2,1,0:T(1,128)}, u32[]{:S(2)}) copy-start(f32[3,1,128,1,256]{4,3,2,1,0:T(1,128)} %param.9) | copy-start | bytes 1179652
  1.4 0.7 %copy-start = (f32[16,3,1,128]{3,2,1,0:T(1,128)S(1)}, f32[16,3,1,128]{3,2,1,0:T(1,128)}, u32[]{:S(2)}) copy-start(f32[16,3,1,128]{3,2,1,0:T(1,128)} %param.5) | copy-start | bytes 73732
  1.4 0.7 %copy-start.1 = (f32[16,256]{1,0:T(8,128)S(1)}, f32[16,256]{1,0:T(8,128)}, u32[]{:S(2)}) copy-start(f32[16,256]{1,0:T(8,128)} %new_ref.1) | copy-start | bytes 49156
  1.4 0.7 %copy-start.2 = (f32[16]{0:T(128)S(1)}, f32[16]{0:T(128)}, u32[]{:S(2)}) copy-start(f32[16]{0:T(128)} %param.7) | copy-start | bytes 196

commit v3 on v2

--- a/solution.py
+++ b/solution.py
@@ -127,14 +127,6 @@
     copies[1].start()
     for k in range(1, panels):
         split_inverse(k)
-    order = []
-    for b, (k, j) in enumerate(below):
-        if j == 0:
-            order.append(1 + k)
-        order.append(1 + panels + b)
-    for number in order:
-        copies[number].start()
-
     for k in range(1, panels):
         k_ref[k] = kernel_rows(panel_points(train_ref, k))
 
@@ -192,12 +184,10 @@
             source = rows(dt * n_col + (col + dc) % n_col)
             send(2, k, h, s_buf.at[k, h, source], s_in.at[k, h, rows(number)], device)
 
-    def look_ahead(k, h):
-        x = x_buf[k, h]
-        for later in range(k + 2, panels):
-            b = below.index((later, k))
-            change = dot_split(l_high[b], l_low[b], x)
-            acc[later, h] = change + acc[later, h] if k > 0 else change
+    def add_earlier(k, j, h):
+        b = below.index((k + 1, j))
+        change = dot_split(l_high[b], l_low[b], x_buf[j, h])
+        acc[k + 1, h] = change + acc[k + 1, h] if j > 0 else change
 
     def sum_residual(k, h):
         wait(s_in.at[k, h, q_rows], recv_sem.at[sem_of(2, k, h)])
@@ -215,17 +205,21 @@
         for h in range(HALVES):
             apply_inverse(k, h)
         if k < panels - 1:
-            take_block(below.index((k + 1, k)))
+            for j in range(k, -1, -1):
+                copies[1 + panels + below.index((k + 1, j))].start()
         for h in range(HALVES):
             sum_solved(k, h)
+        if k < panels - 1:
+            copies[1 + k + 1].start()
+            for j in range(k, -1, -1):
+                take_block(below.index((k + 1, j)))
+            for j in range(k):
+                for h in range(HALVES):
+                    add_earlier(k, j, h)
         if k < panels - 1:
             for h in range(HALVES):
                 apply_factor(k, h)
             take_inverse(k + 1)
-            for later in range(k + 2, panels):
-                take_block(below.index((later, k)))
-            for h in range(HALVES):
-                look_ahead(k, h)
             for h in range(HALVES):
                 sum_residual(k, h)
 

time: 51 us -> 51.2 us (level)
  no operation moved by 1% of the time
where the time goes in v3:
time: 51.2 us; the launch traced here: 51 us
  Pallas kernels  48.2 us (94%)
  local copies, waits for them, and re-layouts  2.65 us (5%)
    pallas_call x1, Pallas kernels, on_device(): pl.pallas_call(functools.partial(kernel, n_row, n_col, panels, dims, unit...  48.2 us
    slice x1, local copies, waits for them, and re-layouts, on_device(): lower = jnp.stack([factor[k, 0, :, j, 0, :] for k, j in below])  1.35 us
    unnamed x11, local copies, waits for them, and re-layouts  1.28 us

profile of v3, /device:TPU:0, one launch (start us, length us, event | category | flops | bytes accessed | tf_op | source)
XLA Modules:
  0.0 51.0 jit_solution(11538294347831361539)
XLA Ops:
  0.0 0.0 copy-start.3
  0.0 1.4 %fusion = (f32[1,1,128,1,1,256]{5,4,3,2,1,0:T(1,128)S(1)}, f32[1,1,128,1,1,256]{5,4,3,2,1,0:T(1,128)S(1)}, f32[1,1,128,1,1,256]{5,4,3,2,1,0:T(1,128)S(1)}) fusion(f32[3,1,128,3,1,256]{5,4,3,2,1,0:T(1,128)} %param.8), kind=kLoop, calls=%fused_computation.5 | loop fusion | bytes 786432 | tf_op jit(solution)/shard_map/slice | solution.py:247
  1.4 0.0 copy-start
  1.4 0.0 copy-start.1
  1.4 0.0 copy-start.2
  1.5 0.0 copy-done.3
  1.5 0.6 %copy-done = f32[16,3,1,128]{3,2,1,0:T(1,128)S(1)} copy-done((f32[16,3,1,128]{3,2,1,0:T(1,128)S(1)}, f32[16,3,1,128]{3,2,1,0:T(1,128)}, u32[]{:S(2)}) %copy-start) | copy-done | bytes 24600
  2.1 0.0 copy-done.1
  2.1 0.0 copy-done.2
  2.1 48.2 %shard_map.55 = f32[3,32,256]{2,1,0:T(8,128)S(1)} custom-call(f32[48,128]{1,0:T(8,128)S(1)} %bitcast.17, f32[16,256]{1,0:T(8,128)S(1)} %copy-done.1, f32[1,16]{1,0:T(1,128)S(1)} %bitcast.18, f32[3,128,256]{2,1,0:T(8,128)S(1)} %pad_maximum_fusion.l_ref, f32[3,128,256]{2,1,0:T(8,128)S(1)} %bitcast.15), custom_call_target="tpu_custom_call" | custom-call | flops 301989888 | bytes 3145728 | tf_op jit(solution)/shard_map/pallas_call | solution.py:272
  50.3 0.6 %copy.21 = f32[3,1,1,32,256]{4,3,2,1,0:T(8,128)} copy(f32[3,1,1,32,256]{4,3,2,1,0:T(8,128)S(1)} %bitcast.16) | data formatting | bytes 196608
  (4 shorter events, 0.1 us)
Async XLA Ops:
  0.0 1.5 %copy-start.3 = (f32[3,1,128,1,256]{4,3,2,1,0:T(1,128)S(1)}, f32[3,1,128,1,256]{4,3,2,1,0:T(1,128)}, u32[]{:S(2)}) copy-start(f32[3,1,128,1,256]{4,3,2,1,0:T(1,128)} %param.9) | copy-start | bytes 1179652
  1.4 0.7 %copy-start = (f32[16,3,1,128]{3,2,1,0:T(1,128)S(1)}, f32[16,3,1,128]{3,2,1,0:T(1,128)}, u32[]{:S(2)}) copy-start(f32[16,3,1,128]{3,2,1,0:T(1,128)} %param.5) | copy-start | bytes 73732
  1.4 0.7 %copy-start.1 = (f32[16,256]{1,0:T(8,128)S(1)}, f32[16,256]{1,0:T(8,128)}, u32[]{:S(2)}) copy-start(f32[16,256]{1,0:T(8,128)} %new_ref.1) | copy-start | bytes 49156
  1.4 0.7 %copy-start.2 = (f32[16]{0:T(128)S(1)}, f32[16]{0:T(128)}, u32[]{:S(2)}) copy-start(f32[16]{0:T(128)} %param.7) | copy-start | bytes 196

commit v4 on v3

--- a/solution.py
+++ b/solution.py
@@ -10,6 +10,7 @@
 MESH = pl.DeviceIdType.MESH
 HIGHEST = lax.Precision.HIGHEST
 HALVES = 2
+LAG = 2
 
 
 def dot(a, b):
@@ -128,6 +129,10 @@
     for k in range(1, panels):
         split_inverse(k)
     for k in range(1, panels):
+        for j in range(k - 1, -1, -1):
+            copies[1 + panels + below.index((k, j))].start()
+        copies[1 + k].start()
+    for k in range(1, panels):
         k_ref[k] = kernel_rows(panel_points(train_ref, k))
 
     for k in range(panels - 1):
@@ -200,28 +205,26 @@
                 3, k, h, r_buf.at[k + 1, h, rows(col)], r_buf.at[k + 1, h, rows(dt * n_col + col)], device
             )
 
-    take_inverse(0)
+    stages = []
     for k in range(panels):
+        stages += [(apply_inverse, k), (sum_solved, k)]
+        if k < panels - 1:
+            stages += [(apply_factor, k), (sum_residual, k)]
+    for tick in range(len(stages) + (HALVES - 1) * LAG):
         for h in range(HALVES):
-            apply_inverse(k, h)
-        if k < panels - 1:
-            for j in range(k, -1, -1):
-                copies[1 + panels + below.index((k + 1, j))].start()
-        for h in range(HALVES):
-            sum_solved(k, h)
-        if k < panels - 1:
-            copies[1 + k + 1].start()
-            for j in range(k, -1, -1):
-                take_block(below.index((k + 1, j)))
-            for j in range(k):
-                for h in range(HALVES):
-                    add_earlier(k, j, h)
-        if k < panels - 1:
-            for h in range(HALVES):
-                apply_factor(k, h)
-            take_inverse(k + 1)
-            for h in range(HALVES):
-                sum_residual(k, h)
+            at = tick - h * LAG
+            if not 0 <= at < len(stages):
+                continue
+            stage, k = stages[at]
+            if h == 0 and stage is apply_inverse:
+                take_inverse(k)
+            if stage is apply_factor:
+                for j in range(k, -1, -1):
+                    if h == 0:
+                        take_block(below.index((k + 1, j)))
+                    if j < k:
+                        add_earlier(k, j, h)
+            stage(k, h)
 
     for copy in copies:
         copy.wait_send()

time: 51.2 us -> 56.4 us (1.10)
  Pallas kernels: 48.2 us -> 53.5 us
    pallas_call x1, Pallas kernels: 48.2 us -> 53.5 us  [on_device(): pl.pallas_call(functools.partial(kernel, n_row, n_col, panels, dims, unit...]
where the time goes in v4:
time: 56.4 us; the launch traced here: 56.2 us
  Pallas kernels  53.5 us (95%)
  local copies, waits for them, and re-layouts  2.65 us (5%)
    pallas_call x1, Pallas kernels, on_device(): pl.pallas_call(functools.partial(kernel, n_row, n_col, panels, dims, unit...  53.5 us
    slice x1, local copies, waits for them, and re-layouts, on_device(): lower = jnp.stack([factor[k, 0, :, j, 0, :] for k, j in below])  1.35 us
    unnamed x11, local copies, waits for them, and re-layouts  1.28 us

profile of v4, /device:TPU:0, one launch (start us, length us, event | category | flops | bytes accessed | tf_op | source)
XLA Modules:
  0.0 56.2 jit_solution(14934743622180771190)
XLA Ops:
  0.0 0.0 copy-start.3
  0.0 1.4 %fusion = (f32[1,1,128,1,1,256]{5,4,3,2,1,0:T(1,128)S(1)}, f32[1,1,128,1,1,256]{5,4,3,2,1,0:T(1,128)S(1)}, f32[1,1,128,1,1,256]{5,4,3,2,1,0:T(1,128)S(1)}) fusion(f32[3,1,128,3,1,256]{5,4,3,2,1,0:T(1,128)} %param.8), kind=kLoop, calls=%fused_computation.5 | loop fusion | bytes 786432 | tf_op jit(solution)/shard_map/slice | solution.py:250
  1.4 0.0 copy-start
  1.4 0.0 copy-start.1
  1.4 0.0 copy-start.2
  1.5 0.0 copy-done.3
  1.5 0.6 %copy-done = f32[16,3,1,128]{3,2,1,0:T(1,128)S(1)} copy-done((f32[16,3,1,128]{3,2,1,0:T(1,128)S(1)}, f32[16,3,1,128]{3,2,1,0:T(1,128)}, u32[]{:S(2)}) %copy-start) | copy-done | bytes 24600
  2.1 0.0 copy-done.1
  2.1 0.0 copy-done.2
  2.1 53.5 %shard_map.55 = f32[3,32,256]{2,1,0:T(8,128)S(1)} custom-call(f32[48,128]{1,0:T(8,128)S(1)} %bitcast.17, f32[16,256]{1,0:T(8,128)S(1)} %copy-done.1, f32[1,16]{1,0:T(1,128)S(1)} %bitcast.18, f32[3,128,256]{2,1,0:T(8,128)S(1)} %pad_maximum_fusion.l_ref, f32[3,128,256]{2,1,0:T(8,128)S(1)} %bitcast.15), custom_call_target="tpu_custom_call" | custom-call | flops 301989888 | bytes 3145728 | tf_op jit(solution)/shard_map/pallas_call | solution.py:275
  55.6 0.6 %copy.21 = f32[3,1,1,32,256]{4,3,2,1,0:T(8,128)} copy(f32[3,1,1,32,256]{4,3,2,1,0:T(8,128)S(1)} %bitcast.16) | data formatting | bytes 196608
  (4 shorter events, 0.1 us)
Async XLA Ops:
  0.0 1.5 %copy-start.3 = (f32[3,1,128,1,256]{4,3,2,1,0:T(1,128)S(1)}, f32[3,1,128,1,256]{4,3,2,1,0:T(1,128)}, u32[]{:S(2)}) copy-start(f32[3,1,128,1,256]{4,3,2,1,0:T(1,128)} %param.9) | copy-start | bytes 1179652
  1.4 0.7 %copy-start = (f32[16,3,1,128]{3,2,1,0:T(1,128)S(1)}, f32[16,3,1,128]{3,2,1,0:T(1,128)}, u32[]{:S(2)}) copy-start(f32[16,3,1,128]{3,2,1,0:T(1,128)} %param.5) | copy-start | bytes 73732
  1.4 0.7 %copy-start.1 = (f32[16,256]{1,0:T(8,128)S(1)}, f32[16,256]{1,0:T(8,128)}, u32[]{:S(2)}) copy-start(f32[16,256]{1,0:T(8,128)} %new_ref.1) | copy-start | bytes 49156
  1.4 0.7 %copy-start.2 = (f32[16]{0:T(128)S(1)}, f32[16]{0:T(128)}, u32[]{:S(2)}) copy-start(f32[16]{0:T(128)} %param.7) | copy-start | bytes 196

commit v5 on v4

--- a/solution.py
+++ b/solution.py
@@ -9,8 +9,8 @@
 
 MESH = pl.DeviceIdType.MESH
 HIGHEST = lax.Precision.HIGHEST
-HALVES = 2
-LAG = 2
+HALVES = 1
+LAG = 0
 
 
 def dot(a, b):

time: 56.4 us -> 55.6 us (0.986)
  Pallas kernels: 53.5 us -> 52.7 us
    pallas_call x1, Pallas kernels: 53.5 us -> 52.7 us  [on_device(): pl.pallas_call(functools.partial(kernel, n_row, n_col, panels, dims, unit...]
where the time goes in v5:
time: 55.6 us; the launch traced here: 55.5 us
  Pallas kernels  52.7 us (95%)
  local copies, waits for them, and re-layouts  2.65 us (5%)
    pallas_call x1, Pallas kernels, on_device(): pl.pallas_call(functools.partial(kernel, n_row, n_col, panels, dims, unit...  52.7 us
    slice x1, local copies, waits for them, and re-layouts, on_device(): lower = jnp.stack([factor[k, 0, :, j, 0, :] for k, j in below])  1.35 us
    unnamed x11, local copies, waits for them, and re-layouts  1.28 us

profile of v5, /device:TPU:0, one launch (start us, length us, event | category | flops | bytes accessed | tf_op | source)
XLA Modules:
  0.0 55.5 jit_solution(8896524694492060085)
XLA Ops:
  0.0 0.0 copy-start.3
  0.0 1.4 %fusion = (f32[1,1,128,1,1,256]{5,4,3,2,1,0:T(1,128)S(1)}, f32[1,1,128,1,1,256]{5,4,3,2,1,0:T(1,128)S(1)}, f32[1,1,128,1,1,256]{5,4,3,2,1,0:T(1,128)S(1)}) fusion(f32[3,1,128,3,1,256]{5,4,3,2,1,0:T(1,128)} %param.8), kind=kLoop, calls=%fused_computation.5 | loop fusion | bytes 786432 | tf_op jit(solution)/shard_map/slice | solution.py:250
  1.4 0.0 copy-start
  1.4 0.0 copy-start.1
  1.4 0.0 copy-start.2
  1.5 0.0 copy-done.3
  1.5 0.6 %copy-done = f32[16,3,1,128]{3,2,1,0:T(1,128)S(1)} copy-done((f32[16,3,1,128]{3,2,1,0:T(1,128)S(1)}, f32[16,3,1,128]{3,2,1,0:T(1,128)}, u32[]{:S(2)}) %copy-start) | copy-done | bytes 24600
  2.1 0.0 copy-done.1
  2.1 0.0 copy-done.2
  2.1 52.7 %shard_map.55 = f32[3,32,256]{2,1,0:T(8,128)S(1)} custom-call(f32[48,128]{1,0:T(8,128)S(1)} %bitcast.17, f32[16,256]{1,0:T(8,128)S(1)} %copy-done.1, f32[1,16]{1,0:T(1,128)S(1)} %bitcast.18, f32[3,128,256]{2,1,0:T(8,128)S(1)} %pad_maximum_fusion.l_ref, f32[3,128,256]{2,1,0:T(8,128)S(1)} %bitcast.15), custom_call_target="tpu_custom_call" | custom-call | flops 301989888 | bytes 3145728 | tf_op jit(solution)/shard_map/pallas_call | solution.py:275
  54.8 0.6 %copy.21 = f32[3,1,1,32,256]{4,3,2,1,0:T(8,128)} copy(f32[3,1,1,32,256]{4,3,2,1,0:T(8,128)S(1)} %bitcast.16) | data formatting | bytes 196608
  (4 shorter events, 0.1 us)
Async XLA Ops:
  0.0 1.5 %copy-start.3 = (f32[3,1,128,1,256]{4,3,2,1,0:T(1,128)S(1)}, f32[3,1,128,1,256]{4,3,2,1,0:T(1,128)}, u32[]{:S(2)}) copy-start(f32[3,1,128,1,256]{4,3,2,1,0:T(1,128)} %param.9) | copy-start | bytes 1179652
  1.4 0.7 %copy-start = (f32[16,3,1,128]{3,2,1,0:T(1,128)S(1)}, f32[16,3,1,128]{3,2,1,0:T(1,128)}, u32[]{:S(2)}) copy-start(f32[16,3,1,128]{3,2,1,0:T(1,128)} %param.5) | copy-start | bytes 73732
  1.4 0.7 %copy-start.1 = (f32[16,256]{1,0:T(8,128)S(1)}, f32[16,256]{1,0:T(8,128)}, u32[]{:S(2)}) copy-start(f32[16,256]{1,0:T(8,128)} %new_ref.1) | copy-start | bytes 49156
  1.4 0.7 %copy-start.2 = (f32[16]{0:T(128)S(1)}, f32[16]{0:T(128)}, u32[]{:S(2)}) copy-start(f32[16]{0:T(128)} %param.7) | copy-start | bytes 196
